TPU v7x, 32 devices: a whole 2x2x4 slice. The times are simulated.
32 devices in a mesh: groups: 2 (over x), node: 16 (over z, y, core).
Axes of the slice: x: 2, y: 2, z: 4, core: 2. Of those that a mesh axis runs over, the one named last changes fastest.
Arguments:
- features: bfloat16 [32768, 1024], P(('groups', 'node')), parts along dimension 0, may hold values from -6 to 6
- filter_gate_weight: bfloat16 [64, 64], replicated, may hold values from -0.75 to 0.75
- skip_weight: bfloat16 [32, 256], replicated, may hold values from -1 to 1
- mix_weight: bfloat16 [96, 32], replicated, may hold values from -0.625 to 0.625
- band_weight: bfloat16 [16384, 192], P('node'), may hold values from -0.4375 to 0.4375
- far_weight: bfloat16 [64, 15360], P(None, 'node'), may hold values from -0.75 to 0.75
- far_ptr: int32 [16, 17], P('node'), may hold values from 0 to 15, as said below
- far_col: int32 [16, 15], P('node'), may hold values from 0 to 31, as said below
- export_block: int32 [16, 2], replicated, may hold values from 0 to 15, as said below
Outputs:
- residual_output: bfloat16 [32768, 512], P(('groups', 'node')), parts along dimension 0
- skip_out: bfloat16 [32768, 4096], P(('groups', 'node')), parts along dimension 0
There are 2 independent parts, one for each index of `groups`. A program takes and returns all parts, laid end to end along the dimension named above; an argument that names none is the same for every part. Nothing has to cross between parts.
Inputs may be any that keep to these rules, and one draw needn't show every extreme that they name: Each row of export_block holds 2 different local block numbers, each below 16. `far_ptr`: each row starts at 0 and never falls; its last entry is the number of used far-block slots of that device, and some device uses all 15. `far_col`: slots below far_ptr[d][16] name blocks of devices other than d, at most one slot for each other device; the other slots hold 0 and belong to no block row. The device that uses all slots reads entry 0 of device 0 and the last entry of the last device.
All inputs are finite; a program needn't handle non-finite values.
Results may differ from a plain program's by a relative error of at most 0.0052.
Values may be sent and summed in bfloat16 or wider, within the bound.
A program may use at most 128 MiB of HBM per device.

v0:
```python
import jax
import jax.numpy as jnp
from jax import lax
from jax.sharding import PartitionSpec as P

BLK = 64
TOUT = 16
DILATION_STEP = 16
EXPORT = 2
CHANNEL_WIDTH = 32
S = 256
TIN = 32


def padded_2(block, sides, width):
    for axis, dim in sides:
        count = lax.axis_size(axis)
        forward = [(i, i + 1) for i in range(count - 1)]
        backward = [(target, source) for source, target in forward]
        low = lax.ppermute(
            lax.slice_in_dim(block, block.shape[dim] - width, None, axis=dim), axis, forward
        )
        high = lax.ppermute(lax.slice_in_dim(block, 0, width, axis=dim), axis, backward)
        block = jnp.concatenate([low, block, high], axis=dim)
    return block


def local(
    features,
    filter_gate_weight,
    skip_weight,
    mix_weight,
    band_weight,
    far_weight,
    far_ptr,
    far_col,
    export_block,
):
    node_rows = features.shape[0]
    blocks = node_rows // BLK
    far_cap = far_col.shape[1]
    peer_count = far_cap + 1
    series_input = features.reshape(node_rows, TIN, CHANNEL_WIDTH)
    preact = jnp.einsum(
        "myv,vi->myi",
        series_input[:, :TOUT],
        filter_gate_weight[:CHANNEL_WIDTH],
        preferred_element_type=jnp.float32,
    )
    preact = preact + jnp.einsum(
        "myv,vi->myi",
        series_input[:, DILATION_STEP:],
        filter_gate_weight[CHANNEL_WIDTH:],
        preferred_element_type=jnp.float32,
    )
    hidden = (
        jnp.tanh(preact[..., :CHANNEL_WIDTH]) * jax.nn.sigmoid(preact[..., CHANNEL_WIDTH:])
    ).astype(jnp.bfloat16)
    skip_out = jnp.einsum(
        "ntc,cs->nts", hidden, skip_weight, preferred_element_type=jnp.float32
    ).astype(jnp.bfloat16)
    skip_out = skip_out.reshape(node_rows, TOUT * S)
    hidden_flat = hidden.reshape(node_rows, TOUT * CHANNEL_WIDTH)
    own_index = lax.axis_index("node")
    own_exports = lax.dynamic_slice_in_dim(export_block, own_index, 1, 0)[0]
    columns = far_col[0]
    sources = columns // EXPORT
    slot_export = columns % EXPORT
    pointers = far_ptr[0]
    slot_ids = jnp.arange(far_cap, dtype=jnp.int32)
    assign = (
        (pointers[:-1, None] <= slot_ids[None, :]) & (slot_ids[None, :] < pointers[1:, None])
    ).astype(jnp.float32)
    weights = far_weight.reshape(BLK, far_cap, BLK).transpose(1, 0, 2)
    band_blocks = band_weight.reshape(blocks, BLK, 3 * BLK)
    in_use = slot_ids < pointers[-1]
    matches = (sources[None, :] == jnp.arange(peer_count, dtype=jnp.int32)[:, None]) & in_use[
        None, :
    ]
    wanted = jnp.sum(jnp.where(matches, slot_export[None, :], 0), axis=1)
    requested = lax.all_to_all(wanted[:, None], "node", split_axis=0, concat_axis=0, tiled=True)[
        :, 0
    ]
    send_rows = own_exports[requested]

    def fetch_far(field_blocks):
        arrived = lax.all_to_all(
            field_blocks[send_rows], "node", split_axis=0, concat_axis=0, tiled=True
        )
        return arrived[sources]

    def diffuse(field_rows):
        padded = padded_2(field_rows, (("node", 0),), BLK)
        padded_blocks = padded.reshape(blocks + 2, BLK, field_rows.shape[1])
        summed = jnp.zeros((blocks, BLK, field_rows.shape[1]), jnp.float32)
        for shift_pos in range(3):
            summed = summed + jnp.einsum(
                "rij,rjm->rim",
                band_blocks[:, :, shift_pos * BLK : (shift_pos + 1) * BLK],
                padded_blocks[shift_pos : shift_pos + blocks],
                preferred_element_type=jnp.float32,
            )
        pieces = fetch_far(field_rows.reshape(blocks, BLK, field_rows.shape[1]))
        products = jnp.einsum("kij,kjm->kim", weights, pieces, preferred_element_type=jnp.float32)
        summed = summed + jnp.einsum(
            "rk,kim->rim", assign, products, precision=lax.Precision.HIGHEST
        )
        return summed.reshape(node_rows, field_rows.shape[1]).astype(jnp.bfloat16)

    hop_one = diffuse(hidden_flat)
    hop_two = diffuse(hop_one)
    joined = jnp.concatenate(
        [
            hidden,
            hop_one.reshape(node_rows, TOUT, CHANNEL_WIDTH),
            hop_two.reshape(node_rows, TOUT, CHANNEL_WIDTH),
        ],
        axis=-1,
    )
    mixed_output = jnp.einsum("myv,vi->myi", joined, mix_weight, preferred_element_type=jnp.float32)
    residual_output = (series_input[:, DILATION_STEP:].astype(jnp.float32) + mixed_output).astype(
        jnp.bfloat16
    )
    return (residual_output.reshape(node_rows, TOUT * CHANNEL_WIDTH), skip_out)


def solution(mesh):
    placed = (
        P(("groups", "node"), None),
        P(),
        P(),
        P(),
        P("node", None),
        P(None, "node"),
        P("node", None),
        P("node", None),
        P(),
    )
    return jax.shard_map(
        local,
        mesh=mesh,
        in_specs=placed,
        out_specs=(P(("groups", "node"), None), P(("groups", "node"), None)),
        check_vma=False,
    )
```

profile of v0, /device:TPU:1, one launch (start us, length us, event | category | flops | bytes accessed | tf_op | source)
XLA Modules:
  0.0 138.1 jit_solution(6040651337936078330)
XLA Ops:
  0.6 0.0 copy-start
  0.6 1.2 slice.121
  1.9 0.6 iota_compare_fusion.3
  2.5 0.7 fusion.53
  3.2 0.1 select_reduce_fusion
  3.3 0.7 copy.73
  4.0 7.3 %all-to-all-start = ((s32[16,1,1]{2,1,0:T(1,128)}), s32[16,1,1]{2,1,0:T(1,128)S(1)}, u32[]{:S(2)}, u32[]{:S(2)}) async-start(s32[16,1,1]{2,1,0:T(1,128)} %copy.73), calls=%async_computation | async-start | bytes 16384 | tf_op jit(solution)/shard_map/all_to_all | solution.py:81
  11.4 0.7 constant_dynamic-slice_fusion
  12.1 0.6 fusion.56
  12.7 2.9 %copy.68 = bf16[1024,1024]{0,1:T(8,128)(2,1)S(1)} copy(bf16[1024,1024]{1,0:T(8,128)(2,1)} %param.9) | data formatting | bytes 4194304 | tf_op args[0]
  15.6 0.8 fusion.37
  16.4 0.6 copy-done.2
  16.9 1.2 convolution_add_fusion
  18.1 0.8 fusion.16
  19.0 2.3 %slice.112 = bf16[16,64,512]{1,0,2:T(8,128)(2,1)} reshape(bf16[1024,16,32]{0,2,1:T(8,128)(2,1)S(1)} %fusion.16) | data formatting | bytes 2097152 | tf_op jit(solution)/shard_map/slice | solution.py:100
  21.3 2.5 %copy.71 = bf16[16,64,512]{2,1,0:T(8,128)(2,1)S(1)} copy(bf16[16,64,512]{1,0,2:T(8,128)(2,1)} %slice.112) | data formatting | bytes 2097152 | tf_op jit(solution)/shard_map/slice | solution.py:100
  23.8 0.0 all-to-all-done
  23.8 0.4 reduce
  24.2 1.3 fusion.51
  25.5 0.0 copy-start.13
  25.5 0.0 copy-start.12
  25.5 1.6 %gather_fusion = bf16[16,64,512]{2,1,0:T(8,128)(2,1)} fusion(bf16[16,64,512]{2,1,0:T(8,128)(2,1)S(1)} %copy.71, s32[1024]{0:T(1024)S(1)} %pad_clamp_fusion.1), kind=kCustom, calls=%fused_computation | custom fusion | bytes 2097216 | tf_op jit(solution)/shard_map/gather | solution.py:88
  27.1 6.0 %all-to-all-start.1 = ((bf16[16,64,512]{2,1,0:T(8,128)(2,1)}), bf16[16,64,512]{2,1,0:T(8,128)(2,1)}, u32[]{:S(2)}, u32[]{:S(2)}) async-start(bf16[16,64,512]{2,1,0:T(8,128)(2,1)} %gather_fusion), calls=%async_computation.1 | async-start | bytes 2097152 | tf_op jit(solution)/shard_map/all_to_all | solution.py:87
  33.1 0.8 fusion.55
  33.9 3.5 %collective-permute-start = (bf16[64,512]{0,1:T(8,128)(2,1)}, bf16[64,512]{0,1:T(8,128)(2,1)}, u32[]{:S(2)}, u32[]{:S(2)}) collective-permute-start(bf16[64,512]{0,1:T(8,128)(2,1)} %bitcast.3), channel_id=1, source_target_pairs={{0,1},{1,2},{2,3},{3,4},{4,5},{5,6},{6,7},{7,8},{8,9},{9,10},{10,1... | collective-permute-start | bytes 196616 | tf_op jit(solution)/shard_map/ppermute | solution.py:20
  37.4 2.1 %collective-permute-start.1 = (bf16[64,512]{0,1:T(8,128)(2,1)S(1)}, bf16[64,512]{0,1:T(8,128)(2,1)}, u32[]{:S(2)}, u32[]{:S(2)}) collective-permute-start(bf16[64,512]{0,1:T(8,128)(2,1)S(1)} %bitcast.109), channel_id=1, source_target_pairs={{1,0},{2,1},{3,2},{4,3},{5,4},{6,5},{7,6},{8,7},{9,8},{10,9},{11,1... | collective-permute-start | bytes 196616 | tf_op jit(solution)/shard_map/ppermute | solution.py:23
  39.5 0.2 reshape.182
  39.8 0.2 copy.70
  40.0 0.7 fusion.52
  40.7 0.8 slice_bitcast_fusion.3
  41.5 1.8 %fusion.24 = f32[16,512,64]{1,2,0:T(8,128)} fusion(bf16[16,64,512]{2,1,0:T(8,128)(2,1)S(1)} %copy.71, bf16[16,64,192]{2,1,0:T(8,128)(2,1)S(1)} %bitcast.96), kind=kOutput, calls=%fused_computation.37 | convolution fusion | flops 67108864 | bytes 3407872 | tf_op jit(solution)/shard_map/rij,rjm->rim/dot_general | solution.py:97
  43.3 0.0 collective-permute-done
  43.3 1.5 %collective-permute-done.1 = bf16[64,512]{0,1:T(8,128)(2,1)} collective-permute-done((bf16[64,512]{0,1:T(8,128)(2,1)S(1)}, bf16[64,512]{0,1:T(8,128)(2,1)}, u32[]{:S(2)}, u32[]{:S(2)}) %collective-permute-start.1) | collective-permute-done | bytes 65568 | tf_op jit(solution)/shard_map/ppermute | solution.py:23
  44.8 3.0 %pad_maximum_fusion.2 = (bf16[1024,512]{0,1:T(8,128)(2,1)}, bf16[1024,512]{0,1:T(8,128)(2,1)S(1)}) fusion(bf16[64,512]{0,1:T(8,128)(2,1)} %collective-permute-done.1, bf16[1024,512]{0,1:T(8,128)(2,1)S(1)} %bitcast.92, bf16[64,512]{0,1:T(8,128)(2,1)} %collective-permute-done), kind=kLoop, calls=%fused_computation.32 | loop fusion | flops 4194304 | bytes 3276800 | tf_op jit(solution)/shard_map/concatenate | solution.py:24
  47.8 2.3 %copy.72 = bf16[1024,512]{1,0:T(8,128)(2,1)} copy(bf16[1024,512]{0,1:T(8,128)(2,1)} %get-tuple-element.16) | data formatting | bytes 2097152 | tf_op jit(solution)/shard_map/slice | solution.py:100
  50.1 1.3 copy.69
  51.4 3.0 %fusion.28 = f32[16,512,64]{1,2,0:T(8,128)} fusion(bf16[16,64,512]{2,1,0:T(8,128)(2,1)} %bitcast.105, bf16[16,64,192]{2,1,0:T(8,128)(2,1)S(1)} %bitcast.97), kind=kOutput, calls=%fused_computation.41 | convolution fusion | flops 67108864 | bytes 3407872 | tf_op jit(solution)/shard_map/rij,rjm->rim/dot_general | solution.py:97
  54.4 1.9 %all-to-all-done.1 = bf16[16,64,512]{2,1,0:T(8,128)(2,1)} async-done(((bf16[16,64,512]{2,1,0:T(8,128)(2,1)}), bf16[16,64,512]{2,1,0:T(8,128)(2,1)}, u32[]{:S(2)}, u32[]{:S(2)}) %all-to-all-start.1) | async-done | bytes 1048608 | tf_op jit(solution)/shard_map/all_to_all | solution.py:87
  56.4 1.8 %gather_fusion.1 = bf16[15,64,512]{2,1,0:T(8,128)(2,1)S(1)} fusion(bf16[16,64,512]{2,1,0:T(8,128)(2,1)} %all-to-all-done.1, s32[1024]{0:T(1024)S(1)} %pad_clamp_fusion), kind=kCustom, calls=%fused_computation.1 | custom fusion | bytes 1966140 | tf_op jit(solution)/shard_map/gather | solution.py:90
  58.2 0.4 convolution_bitcast_fusion.1
  58.6 0.0 copy-start.6
  58.6 2.2 %fusion.14 = f32[16,64,512]{2,0,1:T(8,128)S(1)} fusion(f32[15,64,512]{2,1,0:T(8,128)S(1)} %convolution_bitcast_fusion.1, s32[16]{0:T(128)S(1)} %get-tuple-element.23, s32[16]{0:T(128)S(1)} %get-tuple-element.22), kind=kOutput, calls=%fused_computation.24 | convolution fusion | flops 94372560 | bytes 4063360 | tf_op jit(solution)/shard_map/rk,kim->rim/dot_general | solution.py:105
  60.9 0.0 copy-done.6
  60.9 1.4 %fusion.11 = bf16[16,64,512]{2,1,0:T(8,128)(2,1)S(1)} fusion(f32[16,64,512]{2,0,1:T(8,128)S(1)} %fusion.14, f32[16,512,64]{1,2,0:T(8,128)S(1)} %copy-done.6, f32[16,512,64]{1,2,0:T(8,128)S(1)} %copy-done.5, bf16[16,64,512]{2,1,0:T(8,128)(2,1)S(1)} %bitcast.103, bf16[16,64,192]{2,1,0:T(8,128)(2,1)S(1)} %bitcast.98), kind=kOutput, calls=%fused_computation.21 | convolution fusion | flops 69206016 | bytes 8650752 | tf_op jit(solution)/shard_map/rij,rjm->rim/dot_general | solution.py:97
  62.4 1.7 %gather_fusion.2 = bf16[16,64,512]{2,1,0:T(8,128)(2,1)} fusion(bf16[16,64,512]{2,1,0:T(8,128)(2,1)S(1)} %fusion.11, s32[1024]{0:T(1024)} %copy-done.16), kind=kCustom, calls=%fused_computation.2 | custom fusion | bytes 2097216 | tf_op jit(solution)/shard_map/gather | solution.py:88
  64.1 17.2 %all-to-all-start.2 = ((bf16[16,64,512]{2,1,0:T(8,128)(2,1)}), bf16[16,64,512]{2,1,0:T(8,128)(2,1)}, u32[]{:S(2)}, u32[]{:S(2)}) async-start(bf16[16,64,512]{2,1,0:T(8,128)(2,1)} %gather_fusion.2), calls=%async_computation.2 | async-start | bytes 2097152 | tf_op jit(solution)/shard_map/all_to_all | solution.py:87
  81.3 5.9 %convolution_convert_fusion = bf16[1024,16,256]{0,2,1:T(8,128)(2,1)} fusion(bf16[1024,16,32]{0,2,1:T(8,128)(2,1)S(1)} %fusion.16, bf16[32,256]{1,0:T(8,128)(2,1)S(1)} %copy-done), kind=kOutput, calls=%fused_computation.4 | convolution fusion | flops 272629760 | bytes 9453568 | tf_op jit(solution)/shard_map/ntc,cs->nts/dot_general | solution.py:59
  87.2 11.9 %copy.84 = bf16[1024,4096]{1,0:T(8,128)(2,1)} copy(bf16[1024,4096]{0,1:T(8,128)(2,1)} %bitcast.90) | data formatting | bytes 16777216
  99.1 2.1 %collective-permute-start.3 = (bf16[64,512]{1,0:T(8,128)(2,1)S(1)}, bf16[64,512]{1,0:T(8,128)(2,1)S(1)}, u32[]{:S(2)}, u32[]{:S(2)}) collective-permute-start(bf16[64,512]{1,0:T(8,128)(2,1)S(1)} %get-tuple-element.14), channel_id=1, source_target_pairs={{1,0},{2,1},{3,2},{4,3},{5,4},{6,5},{7,6},{8,7},{9,8},{10,9},{11,1... | collective-permute-start | bytes 196616 | tf_op jit(solution)/shard_map/ppermute | solution.py:23
  101.2 3.7 %collective-permute-start.2 = (bf16[64,512]{1,0:T(8,128)(2,1)S(1)}, bf16[64,512]{1,0:T(8,128)(2,1)S(1)}, u32[]{:S(2)}, u32[]{:S(2)}) collective-permute-start(bf16[64,512]{1,0:T(8,128)(2,1)S(1)} %get-tuple-element.15), channel_id=1, source_target_pairs={{0,1},{1,2},{2,3},{3,4},{4,5},{5,6},{6,7},{7,8},{8,9},{9,10},{10,1... | collective-permute-start | bytes 196616 | tf_op jit(solution)/shard_map/ppermute | solution.py:20
  104.9 1.8 %fusion.26 = f32[16,512,64]{1,2,0:T(8,128)} fusion(bf16[16,64,512]{2,1,0:T(8,128)(2,1)S(1)} %fusion.11, bf16[16,64,192]{2,1,0:T(8,128)(2,1)S(1)} %bitcast.99), kind=kOutput, calls=%fused_computation.39 | convolution fusion | flops 67108864 | bytes 3407872 | tf_op jit(solution)/shard_map/rij,rjm->rim/dot_general | solution.py:97
  106.8 2.8 %copy.78 = bf16[16,64,512]{1,0,2:T(8,128)(2,1)} copy(bf16[16,64,512]{2,1,0:T(8,128)(2,1)S(1)} %fusion.11) | data formatting | bytes 2097152 | tf_op jit(solution)/shard_map/convert_element_type | solution.py:108
  109.6 4.1 %convert_element_type.35 = bf16[1024,16,32]{0,2,1:T(8,128)(2,1)} reshape(bf16[16,64,512]{1,0,2:T(8,128)(2,1)} %copy.78) | data formatting | bytes 2097152 | tf_op jit(solution)/shard_map/convert_element_type | solution.py:108
  113.7 1.1 pad_maximum_fusion
  114.9 0.4 fusion.30
  115.3 0.0 all-to-all-done.2
  115.3 2.9 %gather_fusion.3 = bf16[15,64,512]{2,1,0:T(8,128)(2,1)} fusion(bf16[16,64,512]{2,1,0:T(8,128)(2,1)} %all-to-all-done.2, s32[1024]{0:T(1024)} %copy-done.15), kind=kCustom, calls=%fused_computation.3 | custom fusion | bytes 1966140 | tf_op jit(solution)/shard_map/gather | solution.py:90
  118.2 1.6 %convolution_bitcast_fusion = f32[15,64,512]{2,1,0:T(8,128)S(1)} fusion(bf16[15,64,512]{2,1,0:T(8,128)(2,1)} %gather_fusion.3, bf16[15,64,64]{2,0,1:T(8,128)(2,1)S(1)} %bitcast.107), kind=kOutput, calls=%fused_computation.28 | convolution fusion | flops 62914560 | bytes 3072000 | tf_op jit(solution)/shard_map/kij,kjm->kim/dot_general | solution.py:104
  119.9 2.2 %fusion.12 = f32[16,64,512]{2,0,1:T(8,128)S(1)} fusion(f32[15,64,512]{2,1,0:T(8,128)S(1)} %convolution_bitcast_fusion, s32[16]{0:T(128)S(1)} %copy-done.20, s32[16]{0:T(128)S(1)} %copy-done.18), kind=kOutput, calls=%fused_computation.22 | convolution fusion | flops 94372560 | bytes 4063360 | tf_op jit(solution)/shard_map/rk,kim->rim/dot_general | solution.py:105
  122.1 2.5 %fusion.10 = bf16[16,64,512]{2,1,0:T(8,128)(2,1)} fusion(f32[16,64,512]{2,0,1:T(8,128)S(1)} %fusion.12, f32[16,512,64]{1,2,0:T(8,128)S(1)} %fusion.30, f32[16,512,64]{1,2,0:T(8,128)S(1)} %copy-done.4, bf16[16,64,512]{2,1,0:T(8,128)(2,1)S(1)} %bitcast.102, bf16[16,64,192]{2,1,0:T(8,128)(2,1)S(1)} %bitcast.101), kind=kOutput, calls=%fused_computation.19 | convolution fusion | flops 69206016 | bytes 8650752 | tf_op jit(solution)/shard_map/rij,rjm->rim/dot_general | solution.py:97
  124.7 3.8 %copy.82 = bf16[16,64,512]{1,0,2:T(8,128)(2,1)} copy(bf16[16,64,512]{2,1,0:T(8,128)(2,1)} %fusion.10) | data formatting | bytes 2097152 | tf_op jit(solution)/shard_map/convert_element_type | solution.py:108
  128.5 4.2 %convert_element_type.38 = bf16[1024,16,32]{0,2,1:T(8,128)(2,1)} reshape(bf16[16,64,512]{1,0,2:T(8,128)(2,1)} %copy.82) | data formatting | bytes 2097152 | tf_op jit(solution)/shard_map/convert_element_type | solution.py:108
  132.7 3.1 %add_convert_fusion = bf16[1024,16,32]{0,2,1:T(8,128)(2,1)} fusion(bf16[1024,16,32]{0,2,1:T(8,128)(2,1)} %convert_element_type.38, bf16[1024,16,32]{0,2,1:T(8,128)(2,1)} %convert_element_type.35, bf16[1024,16,32]{0,2,1:T(8,128)(2,1)S(1)} %fusion.16, bf16[1024,32,32]{0,2,1:T(8,128)(2,1)S(1)} %bitcast.95, bf16[96,32]{0,1:T(8,128)(2,1)S(1)} %copy-done.21), kind=kOutput, calls=%fused_computation.26 | convolution fusion | flops 111673344 | bytes 5249024 | tf_op jit(solution)/shard_map/myv,vi->myi/dot_general | solution.py:120
  135.8 2.3 %copy.83 = bf16[1024,512]{1,0:T(8,128)(2,1)} copy(bf16[1024,512]{0,1:T(8,128)(2,1)} %bitcast.108) | data formatting | bytes 2097152
  (43 shorter events, 0.1 us)
Async XLA Ops:
  0.6 80.7 %copy-start = (bf16[32,256]{1,0:T(8,128)(2,1)S(1)}, bf16[32,256]{1,0:T(8,128)(2,1)}, u32[]{:S(2)}) copy-start(bf16[32,256]{1,0:T(8,128)(2,1)} %param.11) | copy-start | bytes 49156
  4.0 19.8 %all-to-all-start = ((s32[16,1,1]{2,1,0:T(1,128)}), s32[16,1,1]{2,1,0:T(1,128)S(1)}, u32[]{:S(2)}, u32[]{:S(2)}) async-start(s32[16,1,1]{2,1,0:T(1,128)} %copy.73), calls=%async_computation | async-start | bytes 16384 | tf_op jit(solution)/shard_map/all_to_all | solution.py:81
  12.7 2.9 %copy-start.14 = (bf16[64,64]{1,0:T(8,128)(2,1)S(1)}, bf16[64,64]{1,0:T(8,128)(2,1)}, u32[]{:S(2)}) copy-start(bf16[64,64]{1,0:T(8,128)(2,1)} %param.10) | copy-start | bytes 24580
  15.6 1.4 copy-start.2
  25.5 1.6 %copy-start.16 = (s32[1024]{0:T(1024)}, s32[1024]{0:T(1024)S(1)}, u32[]{:S(2)}) copy-start(s32[1024]{0:T(1024)S(1)} %pad_clamp_fusion.1) | copy-start | bytes 12292
  25.5 14.0 %copy-start.13 = (bf16[64,960]{1,0:T(8,128)(2,1)S(1)}, bf16[64,960]{1,0:T(8,128)(2,1)}, u32[]{:S(2)}) copy-start(bf16[64,960]{1,0:T(8,128)(2,1)} %param.14) | copy-start | bytes 368644
  25.5 14.3 %copy-start.12 = (bf16[1024,192]{0,1:T(8,128)(2,1)S(1)}, bf16[1024,192]{0,1:T(8,128)(2,1)}, u32[]{:S(2)}) copy-start(bf16[1024,192]{0,1:T(8,128)(2,1)} %param.13) | copy-start | bytes 1179652
  27.1 29.3 %all-to-all-start.1 = ((bf16[16,64,512]{2,1,0:T(8,128)(2,1)}), bf16[16,64,512]{2,1,0:T(8,128)(2,1)}, u32[]{:S(2)}, u32[]{:S(2)}) async-start(bf16[16,64,512]{2,1,0:T(8,128)(2,1)} %gather_fusion), calls=%async_computation.1 | async-start | bytes 2097152 | tf_op jit(solution)/shard_map/all_to_all | solution.py:87
  33.9 9.5 %collective-permute-start = (bf16[64,512]{0,1:T(8,128)(2,1)}, bf16[64,512]{0,1:T(8,128)(2,1)}, u32[]{:S(2)}, u32[]{:S(2)}) collective-permute-start(bf16[64,512]{0,1:T(8,128)(2,1)} %bitcast.3), channel_id=1, source_target_pairs={{0,1},{1,2},{2,3},{3,4},{4,5},{5,6},{6,7},{7,8},{8,9},{9,10},{10,1... | collective-permute-start | bytes 196616 | tf_op jit(solution)/shard_map/ppermute | solution.py:20
  37.4 7.4 %collective-permute-start.1 = (bf16[64,512]{0,1:T(8,128)(2,1)S(1)}, bf16[64,512]{0,1:T(8,128)(2,1)}, u32[]{:S(2)}, u32[]{:S(2)}) collective-permute-start(bf16[64,512]{0,1:T(8,128)(2,1)S(1)} %bitcast.109), channel_id=1, source_target_pairs={{1,0},{2,1},{3,2},{4,3},{5,4},{6,5},{7,6},{8,7},{9,8},{10,9},{11,1... | collective-permute-start | bytes 196616 | tf_op jit(solution)/shard_map/ppermute | solution.py:23
  40.0 65.0 %copy-start.7 = (bf16[1024,192]{1,0:T(8,128)(2,1)}, bf16[1024,192]{1,0:T(8,128)(2,1)S(1)}, u32[]{:S(2)}) copy-start(bf16[1024,192]{1,0:T(8,128)(2,1)S(1)} %copy.70) | copy-start | bytes 1179652
  41.5 17.1 %copy-start.17 = (s32[16]{0:T(128)}, s32[16]{0:T(128)S(1)}, u32[]{:S(2)}) copy-start(s32[16]{0:T(128)S(1)} %get-tuple-element.22) | copy-start | bytes 196
  41.5 17.1 %copy-start.19 = (s32[16]{0:T(128)}, s32[16]{0:T(128)S(1)}, u32[]{:S(2)}) copy-start(s32[16]{0:T(128)S(1)} %get-tuple-element.23) | copy-start | bytes 196
  43.3 13.0 %copy-start.15 = (s32[1024]{0:T(1024)}, s32[1024]{0:T(1024)S(1)}, u32[]{:S(2)}) copy-start(s32[1024]{0:T(1024)S(1)} %pad_clamp_fusion) | copy-start | bytes 12292
  58.2 2.7 %copy-start.11 = (bf16[1024,512]{1,0:T(8,128)(2,1)S(1)}, bf16[1024,512]{1,0:T(8,128)(2,1)}, u32[]{:S(2)}) copy-start(bf16[1024,512]{1,0:T(8,128)(2,1)} %copy.72) | copy-start | bytes 3145732
  58.6 2.3 %copy-start.5 = (f32[16,512,64]{1,2,0:T(8,128)S(1)}, f32[16,512,64]{1,2,0:T(8,128)}, u32[]{:S(2)}) copy-start(f32[16,512,64]{1,2,0:T(8,128)} %fusion.24) | copy-start | bytes 6291460
  58.6 2.3 %copy-start.6 = (f32[16,512,64]{1,2,0:T(8,128)S(1)}, f32[16,512,64]{1,2,0:T(8,128)}, u32[]{:S(2)}) copy-start(f32[16,512,64]{1,2,0:T(8,128)} %fusion.28) | copy-start | bytes 6291460
  64.1 51.2 %all-to-all-start.2 = ((bf16[16,64,512]{2,1,0:T(8,128)(2,1)}), bf16[16,64,512]{2,1,0:T(8,128)(2,1)}, u32[]{:S(2)}, u32[]{:S(2)}) async-start(bf16[16,64,512]{2,1,0:T(8,128)(2,1)} %gather_fusion.2), calls=%async_computation.2 | async-start | bytes 2097152 | tf_op jit(solution)/shard_map/all_to_all | solution.py:87
  99.1 14.6 %collective-permute-start.3 = (bf16[64,512]{1,0:T(8,128)(2,1)S(1)}, bf16[64,512]{1,0:T(8,128)(2,1)S(1)}, u32[]{:S(2)}, u32[]{:S(2)}) collective-permute-start(bf16[64,512]{1,0:T(8,128)(2,1)S(1)} %get-tuple-element.14), channel_id=1, source_target_pairs={{1,0},{2,1},{3,2},{4,3},{5,4},{6,5},{7,6},{8,7},{9,8},{10,9},{11,1... | collective-permute-start | bytes 196616 | tf_op jit(solution)/shard_map/ppermute | solution.py:23
  101.2 12.5 %collective-permute-start.2 = (bf16[64,512]{1,0:T(8,128)(2,1)S(1)}, bf16[64,512]{1,0:T(8,128)(2,1)S(1)}, u32[]{:S(2)}, u32[]{:S(2)}) collective-permute-start(bf16[64,512]{1,0:T(8,128)(2,1)S(1)} %get-tuple-element.15), channel_id=1, source_target_pairs={{0,1},{1,2},{2,3},{3,4},{4,5},{5,6},{6,7},{7,8},{8,9},{9,10},{10,1... | collective-permute-start | bytes 196616 | tf_op jit(solution)/shard_map/ppermute | solution.py:20
  113.7 1.1 copy-start.8
  115.3 4.5 %copy-start.18 = (s32[16]{0:T(128)S(1)}, s32[16]{0:T(128)}, u32[]{:S(2)}) copy-start(s32[16]{0:T(128)} %copy-done.17) | copy-start | bytes 196
  115.3 4.5 %copy-start.20 = (s32[16]{0:T(128)S(1)}, s32[16]{0:T(128)}, u32[]{:S(2)}) copy-start(s32[16]{0:T(128)} %copy-done.19) | copy-start | bytes 196
  119.8 2.3 %copy-start.4 = (f32[16,512,64]{1,2,0:T(8,128)S(1)}, f32[16,512,64]{1,2,0:T(8,128)}, u32[]{:S(2)}) copy-start(f32[16,512,64]{1,2,0:T(8,128)} %fusion.26) | copy-start | bytes 6291460
  119.9 2.3 %copy-start.9 = (bf16[1024,192]{1,0:T(8,128)(2,1)S(1)}, bf16[1024,192]{1,0:T(8,128)(2,1)}, u32[]{:S(2)}) copy-start(bf16[1024,192]{1,0:T(8,128)(2,1)} %copy-done.7) | copy-start | bytes 1179652
  119.9 2.3 %copy-start.10 = (bf16[1024,512]{1,0:T(8,128)(2,1)S(1)}, bf16[1024,512]{1,0:T(8,128)(2,1)}, u32[]{:S(2)}) copy-start(bf16[1024,512]{1,0:T(8,128)(2,1)} %get-tuple-element.12) | copy-start | bytes 3145732
  128.5 4.2 %copy-start.3 = (bf16[1024,1024]{0,1:T(8,128)(2,1)S(1)}, bf16[1024,1024]{0,1:T(8,128)(2,1)}, u32[]{:S(2)}) copy-start(bf16[1024,1024]{0,1:T(8,128)(2,1)} %copy-done.2) | copy-start | bytes 6291460
  128.5 4.2 %copy-start.21 = (bf16[96,32]{0,1:T(8,128)(2,1)S(1)}, bf16[96,32]{0,1:T(8,128)(2,1)}, u32[]{:S(2)}) copy-start(bf16[96,32]{0,1:T(8,128)(2,1)} %param.12) | copy-start | bytes 18436
  132.7 5.4 %copy-start.1 = (bf16[32,256]{1,0:T(8,128)(2,1)S(1)}, bf16[32,256]{1,0:T(8,128)(2,1)}, u32[]{:S(2)}) copy-start(bf16[32,256]{1,0:T(8,128)(2,1)} %param.11) | copy-start | bytes 49156
where the time goes:
time: 140 us; the launch traced here: 138 us
  local copies, waits for them, and re-layouts  54.4 us (39%)
  starting transfers between devices  42 us (30%)
  matrix products  28.4 us (20%)
  other arithmetic  8.73 us (6%)
  waiting for transfers between devices  3.48 us (2%)
    all_to_all x2, starting transfers between devices, fetch_far(): lax.all_to_all(field_blocks[send_rows], 'node', split_axis=0, concat_axis...  23.3 us
    unnamed x48, local copies, waits for them, and re-layouts  17.9 us
    convert_element_type x4, local copies, waits for them, and re-layouts, diffuse(): return summed.reshape(node_rows, field_rows.shape[1]).astype(jnp.bfloat16)  15 us
    dot_general x6, matrix products, diffuse(): jnp.einsum('rij,rjm->rim', band_blocks[:, :, shift_pos * BLK:(shift_pos +...  11 us
    slice x4, local copies, waits for them, and re-layouts, diffuse(): padded_blocks[shift_pos:shift_pos + blocks]  8.43 us
    all_to_all x1, starting transfers between devices, local(): lax.all_to_all(wanted[:, None], 'node', split_axis=0, concat_axis=0, tile...  7.35 us
    ppermute x2, starting transfers between devices, padded_2(): lax.ppermute(lax.slice_in_dim(block, block.shape[dim] - width, None, axis...  7.25 us
    dot_general x1, matrix products, local(): jnp.einsum('ntc,cs->nts', hidden, skip_weight, preferred_element_type=jnp...  5.9 us
  transfers between devices with their start and end apart: 7, of which 2 were waited for; matrix products, arithmetic and copies ran while one was open for 39% of the time, Pallas kernels for 0%

commit v1 on v0

v1 whole, which is shorter than its diff:
```python
import functools

import jax
import jax.numpy as jnp
from jax import lax
from jax.experimental import pallas as pl
from jax.experimental.pallas import tpu as pltpu
from jax.sharding import PartitionSpec as P

BLK = 64
TOUT = 16
EXPORT = 2
CH = 32
S = 256
PARTS = 2
GROUP = 4
MESH = pl.DeviceIdType.MESH
BF16 = jnp.bfloat16
F32 = jnp.float32


def dot(a, b):
    return jnp.dot(a, b, preferred_element_type=F32)


def one_hot(shape, rule):
    row = lax.broadcasted_iota(jnp.int32, shape, 0)
    col = lax.broadcasted_iota(jnp.int32, shape, 1)
    return jnp.where(rule(row, col), 1.0, 0.0).astype(BF16)


def front_kernel(x_ref, fg_ref, skip_ref, hidden_ref, out_ref, fg_wide, skip_wide):
    lanes = 4 * CH

    @pl.when(pl.program_id(0) == 0)
    def _():
        rows = one_hot((lanes, CH), lambda r, c: r % CH == c)
        spread = one_hot((2 * CH, 2 * lanes), lambda r, c: r == c % CH + CH * (c // lanes))
        keep = one_hot((lanes, 2 * lanes), lambda r, c: r // CH == (c % lanes) // CH)
        for tap in range(2):
            tall = dot(rows, fg_ref[tap * CH : (tap + 1) * CH, :]).astype(BF16)
            fg_wide[tap * lanes : (tap + 1) * lanes, :] = dot(tall, spread).astype(BF16) * keep
        tall = dot(rows, skip_ref[...]).astype(BF16)
        for step in range(4):
            mine = one_hot((lanes, S), lambda r, c: r // CH == step)
            skip_wide[:, step * S : (step + 1) * S] = tall * mine

    for j in range(TOUT // 4):
        early = x_ref[:, j * lanes : (j + 1) * lanes]
        late = x_ref[:, TOUT * CH + j * lanes : TOUT * CH + (j + 1) * lanes]
        pre = dot(jnp.concatenate([early, late], axis=1), fg_wide[...])
        gate = 0.5 * jnp.tanh(0.5 * pre[:, lanes:]) + 0.5
        hidden = (jnp.tanh(pre[:, :lanes]) * gate).astype(BF16)
        hidden_ref[:, j * lanes : (j + 1) * lanes] = hidden
        out_ref[:, j * 4 * S : (j + 1) * 4 * S] = dot(hidden, skip_wide[...]).astype(BF16)


def front(features, fg, skip):
    rows = features.shape[0]
    tile = 128
    return pl.pallas_call(
        front_kernel,
        grid=(rows // tile,),
        in_specs=[
            pl.BlockSpec((tile, features.shape[1]), lambda i: (i, 0)),
            pl.BlockSpec(fg.shape, lambda i: (0, 0)),
            pl.BlockSpec(skip.shape, lambda i: (0, 0)),
        ],
        out_specs=[
            pl.BlockSpec((tile, TOUT * CH), lambda i: (i, 0)),
            pl.BlockSpec((tile, TOUT * S), lambda i: (i, 0)),
        ],
        out_shape=[
            jax.ShapeDtypeStruct((rows, TOUT * CH), BF16),
            jax.ShapeDtypeStruct((rows, TOUT * S), BF16),
        ],
        scratch_shapes=[pltpu.VMEM((8 * CH, 8 * CH), BF16), pltpu.VMEM((4 * CH, 4 * S), BF16)],
        compiler_params=pltpu.CompilerParams(vmem_limit_bytes=32 * 2**20),
        name="front",
    )(features, fg, skip)


def hops_kernel(
    n, zs, ys,
    hid, feat, band, farw, mix, ptr, col, exports,
    out,
    gat_0, gat_1, gat_2, gat_3, halo, fld, pieces, far_mat, band_mat, mix_wide, late, part,
    send_sem, recv_sem, halo_send, halo_recv, local_sem,
):
    rows = hid.shape[0]
    blocks = rows // BLK
    width = hid.shape[1] // PARTS
    slots = col.shape[1]
    gat = [[gat_0, gat_1], [gat_2, gat_3]]
    me = lax.axis_index("node")
    core = me % 2
    y = (me // 2) % ys
    z = me // (2 * ys)

    def index(a, b, c):
        return (a * ys + b) * 2 + c

    z_from = [lax.rem(z + zs - i, zs) for i in range(zs)]
    z_to = [lax.rem(z + i, zs) for i in range(zs)]
    other_y = ys - 1 - y
    across = index(z, other_y, core)
    mate = index(z, y, 1 - core)

    feat_copy = pltpu.make_async_copy(
        feat.at[:, TOUT * CH : 2 * TOUT * CH], late, local_sem.at[0]
    )
    feat_copy.start()

    barrier = pltpu.get_barrier_semaphore()
    greet = [index(z_to[i], y, core) for i in range(1, zs)] + [mate]
    greet += [lax.rem(me + 1, n), lax.rem(me + n - 1, n)]
    if ys > 1:
        greet.append(across)
    for peer in greet:
        pl.semaphore_signal(barrier, inc=1, device_id={"node": peer}, device_id_type=MESH)

    for h in range(PARTS):
        field = hid[:, h * width : (h + 1) * width]
        fld[0, h, 1 : blocks + 1] = field.reshape(blocks, BLK, width)

    def stage(p, h):
        for e in range(EXPORT):
            gat[p][h][me * EXPORT + e] = fld[p, h, exports[me, e] + 1]

    stage(0, 0)
    pl.semaphore_wait(barrier, len(greet))

    def chunk_copy(p, h, source, target, sem):
        return pltpu.make_async_remote_copy(
            src_ref=gat[p][h].at[pl.ds(source * EXPORT, EXPORT)],
            dst_ref=gat[p][h].at[pl.ds(source * EXPORT, EXPORT)],
            send_sem=send_sem.at[p, h, sem],
            recv_sem=recv_sem.at[p, h, source],
            device_id={"node": target},
            device_id_type=MESH,
        )

    def halo_copy(p, h, side, target):
        first = blocks if side == 0 else 1
        return pltpu.make_async_remote_copy(
            src_ref=fld.at[p, h, first],
            dst_ref=halo.at[p, h, side],
            send_sem=halo_send.at[p, h, side],
            recv_sem=halo_recv.at[p, h, side],
            device_id={"node": target},
            device_id_type=MESH,
        )

    y_sems = zs - 1
    mate_sems = y_sems + (zs if ys > 1 else 0)
    sends = []

    def go(p, h, source, target, sem):
        copy = chunk_copy(p, h, source, target, sem)
        copy.start()
        sends.append(copy)

    def arrived(p, h, source):
        chunk_copy(p, h, source, mate, 0).wait_recv()

    def start_own(p, h):
        for i in range(1, zs):
            go(p, h, me, index(z_to[i], y, core), i - 1)
        if ys > 1:
            go(p, h, me, across, y_sems)
        go(p, h, me, mate, mate_sems)

        @pl.when(me < n - 1)
        def _():
            halo_copy(p, h, 0, me + 1).start()

        @pl.when(me > 0)
        def _():
            halo_copy(p, h, 1, me - 1).start()

    def pass_z(p, h):
        for i in range(1, zs):
            source = index(z_from[i], y, core)
            arrived(p, h, source)
            if ys > 1:
                go(p, h, source, across, y_sems + i)
            go(p, h, source, mate, mate_sems + i)

    def pass_y(p, h):
        if ys > 1:
            for i in range(zs):
                source = index(z_from[i], other_y, core)
                arrived(p, h, source)
                go(p, h, source, mate, mate_sems + zs + i)

    def finish(p, h):
        for side_y in [y, other_y][:ys]:
            for i in range(zs):
                arrived(p, h, index(z_from[i], side_y, 1 - core))

        @pl.when(me > 0)
        def _():
            halo_copy(p, h, 0, me - 1).wait_recv()

        @pl.when(me < n - 1)
        def _():
            halo_copy(p, h, 1, me + 1).wait_recv()

        fld[p, h, 0] = halo[p, h, 0]
        fld[p, h, blocks + 1] = halo[p, h, 1]
        for k in range(slots):
            pieces[k * BLK : (k + 1) * BLK, :] = gat[p][h][col[0, k]]

    def diffuse(p, h, g):
        high = GROUP * BLK
        lines = slice(g * high, (g + 1) * high)
        field = fld[p, h, g * GROUP : (g + 1) * GROUP + 2].reshape(high + 2 * BLK, width)
        near = dot(band_mat[lines, :], field)
        return near + dot(far_mat[lines, :], pieces[...])

    def build():
        for r in range(blocks):
            i = r % GROUP
            shift = one_hot((3 * BLK, (GROUP + 2) * BLK), lambda a, b: a + i * BLK == b)
            lines = slice(r * BLK, (r + 1) * BLK)
            band_mat[lines, :] = dot(band[lines, :], shift).astype(BF16)
            slot = lax.broadcasted_iota(jnp.int32, (1, slots * BLK), 1) // BLK
            used = jnp.logical_and(slot >= ptr[0, r], slot < ptr[0, r + 1])
            far_mat[lines, :] = farw[...] * jnp.where(used, 1.0, 0.0).astype(BF16)
        size = mix_wide.shape[1]
        tall_rule = one_hot((size, CH), lambda a, b: a % CH == b)
        wide_rule = one_hot((CH, size), lambda a, b: a == b % CH)
        keep = one_hot((size, size), lambda a, b: a // CH == b // CH)
        for term in range(3):
            tall = dot(tall_rule, mix[term * CH : (term + 1) * CH, :]).astype(BF16)
            mix_wide[term] = dot(tall, wide_rule).astype(BF16) * keep

    def hop_one(h):
        for g in range(blocks // GROUP):
            field = diffuse(0, h, g).astype(BF16).reshape(GROUP, BLK, width)
            fld[1, h, 1 + g * GROUP : 1 + (g + 1) * GROUP] = field

    def mix_early(h):
        columns = slice(h * width, (h + 1) * width)
        part[:, columns] = (
            late[:, columns].astype(F32)
            + dot(fld[0, h, 1 : blocks + 1].reshape(rows, width), mix_wide[0])
            + dot(fld[1, h, 1 : blocks + 1].reshape(rows, width), mix_wide[1])
        )

    def hop_two(h):
        columns = slice(h * width, (h + 1) * width)
        for g in range(blocks // GROUP):
            lines = slice(g * GROUP * BLK, (g + 1) * GROUP * BLK)
            field = diffuse(1, h, g).astype(BF16)
            out[lines, columns] = (part[lines, columns] + dot(field, mix_wide[2])).astype(BF16)

    start_own(0, 0)
    stage(0, 1)
    start_own(0, 1)

    @pl.when(me == 0)
    def _():
        for p in range(2):
            for h in range(PARTS):
                halo[p, h, 0] = jnp.zeros((BLK, width), BF16)

    @pl.when(me == n - 1)
    def _():
        for p in range(2):
            for h in range(PARTS):
                halo[p, h, 1] = jnp.zeros((BLK, width), BF16)

    pass_z(0, 0)
    build()
    feat_copy.wait()
    pass_y(0, 0)
    pass_z(0, 1)
    finish(0, 0)
    hop_one(0)
    stage(1, 0)
    start_own(1, 0)
    pass_y(0, 1)
    pass_z(1, 0)
    finish(0, 1)
    hop_one(1)
    stage(1, 1)
    start_own(1, 1)
    mix_early(0)
    pass_y(1, 0)
    pass_z(1, 1)
    mix_early(1)
    finish(1, 0)
    hop_two(0)
    pass_y(1, 1)
    finish(1, 1)
    hop_two(1)
    for copy in sends:
        copy.wait_send()
    for p in range(2):
        for h in range(PARTS):

            @pl.when(me < n - 1)
            def _():
                halo_copy(p, h, 0, me + 1).wait_send()

            @pl.when(me > 0)
            def _():
                halo_copy(p, h, 1, me - 1).wait_send()


def hops(n, hidden, features, band, farw, mix, ptr, col, exports):
    rows, columns = hidden.shape
    ys = 2 if n == 16 else 1
    zs = n // (2 * ys)
    width = columns // PARTS
    chunk_sends = zs - 1 + (zs if ys > 1 else 0) + zs * ys
    vmem = pl.BlockSpec(memory_space=pltpu.VMEM)
    smem = pl.BlockSpec(memory_space=pltpu.SMEM)
    return pl.pallas_call(
        functools.partial(hops_kernel, n, zs, ys),
        in_specs=[vmem, pl.BlockSpec(memory_space=pl.ANY), vmem, vmem, vmem, smem, smem, smem],
        out_specs=vmem,
        out_shape=jax.ShapeDtypeStruct((rows, columns), BF16),
        scratch_shapes=[
            *[pltpu.VMEM((n * EXPORT, BLK, width), BF16)] * (2 * PARTS),
            pltpu.VMEM((2, PARTS, 2, BLK, width), BF16),
            pltpu.VMEM((2, PARTS, rows // BLK + 2, BLK, width), BF16),
            pltpu.VMEM((farw.shape[1], width), BF16),
            pltpu.VMEM((rows, farw.shape[1]), BF16),
            pltpu.VMEM((rows, (GROUP + 2) * BLK), BF16),
            pltpu.VMEM((3, width, width), BF16),
            pltpu.VMEM((rows, columns), BF16),
            pltpu.VMEM((rows, columns), F32),
            pltpu.SemaphoreType.DMA((2, PARTS, chunk_sends)),
            pltpu.SemaphoreType.DMA((2, PARTS, n)),
            pltpu.SemaphoreType.DMA((2, PARTS, 2)),
            pltpu.SemaphoreType.DMA((2, PARTS, 2)),
            pltpu.SemaphoreType.DMA((1,)),
        ],
        compiler_params=pltpu.CompilerParams(
            collective_id=0, has_side_effects=True, vmem_limit_bytes=52 * 2**20
        ),
        name="hops",
    )(hidden, features, band, farw, mix, ptr, col, exports)


def solution(mesh):
    n = mesh.shape["node"]

    def local(features, fg, skip, mix, band, farw, ptr, col, exports):
        hidden, skip_out = front(features, fg, skip)
        residual = hops(n, hidden, features, band, farw, mix, ptr, col, exports)
        return residual, skip_out

    rows = P(("groups", "node"), None)
    return jax.shard_map(
        local,
        mesh=mesh,
        in_specs=(
            rows, P(), P(), P(), P("node", None), P(None, "node"), P("node", None), P("node", None), P(),
        ),
        out_specs=(rows, rows),
        check_vma=False,
    )
```

time: 140 us -> 65.3 us (0.47); the launches traced: 138 us -> 64.9 us
  Pallas kernels: 0 us -> 54.3 us
  local copies, waits for them, and re-layouts: 54.4 us -> 9.93 us
  starting transfers between devices: 42 us -> 0 us
  matrix products: 28.4 us -> 0 us
  other arithmetic: 8.73 us -> 0 us
  waiting for transfers between devices: 3.48 us -> 0 us
    pallas_call x0 -> x2, Pallas kernels: none -> 54.3 us  [the longest x1 45 us: hops(): pl.pallas_call(functools.partial(hops_kernel, n, zs, ys), in_specs=[vmem,...]
    all_to_all x3 -> x0, starting transfers between devices: 30.6 us -> none  [the longest x2 23.3 us: fetch_far(): lax.all_to_all(field_blocks[send_rows], 'node', split_axis=0, concat_axis...]
    dot_general x14 -> x0, matrix products: 28.4 us -> none  [the longest x6 11 us: diffuse(): jnp.einsum('rij,rjm->rim', band_blocks[:, :, shift_pos * BLK:(shift_pos +...]
    convert_element_type x4 -> x0, local copies, waits for them, and re-layouts: 15 us -> none  [diffuse(): return summed.reshape(node_rows, field_rows.shape[1]).astype(jnp.bfloat16)]
    ppermute x4 -> x0, starting transfers between devices: 11.4 us -> none  [the longest x2 7.25 us: padded_2(): lax.ppermute(lax.slice_in_dim(block, block.shape[dim] - width, None, axis...]
    slice x7 -> x0, local copies, waits for them, and re-layouts: 10.4 us -> none  [the longest x4 8.43 us: diffuse(): padded_blocks[shift_pos:shift_pos + blocks]]
    gather x5 -> x0, local copies, waits for them, and re-layouts: 8.62 us -> none  [the longest x2 4.74 us: fetch_far(): return arrived[sources]]
    unnamed x48 -> x18, local copies, waits for them, and re-layouts: 17.9 us -> 9.93 us
  transfers between devices with their start and end apart: 7 -> 0, of which waited for: 2 -> 0; matrix products, arithmetic and copies ran while one was open for 39% -> 0% of each run, Pallas kernels for 0% -> 0%
where the time goes in v1:
time: 65.3 us; the launch traced here: 64.9 us
  Pallas kernels  54.3 us (83%)
  local copies, waits for them, and re-layouts  9.93 us (15%)
  between operations  0.66 us (1%)
    pallas_call x1, Pallas kernels, hops(): pl.pallas_call(functools.partial(hops_kernel, n, zs, ys), in_specs=[vmem,...  45 us
    unnamed x18, local copies, waits for them, and re-layouts  9.93 us
    pallas_call x1, Pallas kernels, front(): pl.pallas_call(front_kernel, grid=(rows // tile,), in_specs=[pl.BlockSpec...  9.31 us

profile of v1, /device:TPU:1, one launch (start us, length us, event | category | flops | bytes accessed | tf_op | source)
XLA Modules:
  0.0 64.9 jit_solution(14644945016115489005)
XLA Ops:
  0.6 0.8 %copy.13.exports = s32[16,2]{1,0:T(8,128)S(1)} copy(s32[16,2]{0,1:T(2,128)} %param.17) | data formatting | bytes 256 | tf_op args[8]
  1.4 0.8 %copy.12.mix = bf16[96,32]{1,0:T(8,128)(2,1)S(1)} copy(bf16[96,32]{0,1:T(8,128)(2,1)} %param.12) | data formatting | bytes 12288 | tf_op args[3]
  2.2 1.2 %copy.11.band = bf16[1024,192]{1,0:T(8,128)(2,1)S(1)} copy(bf16[1024,192]{0,1:T(8,128)(2,1)} %param.13) | data formatting | bytes 786432 | tf_op args[4]
  3.4 0.0 copy-start
  3.4 1.6 %copy-done = bf16[1024,1024]{1,0:T(8,128)(2,1)S(1)} copy-done((bf16[1024,1024]{1,0:T(8,128)(2,1)S(1)}, bf16[1024,1024]{1,0:T(8,128)(2,1)}, u32[]{:S(2)}) %copy-start) | copy-done | bytes 2097176
  5.0 0.0 copy-start.3
  5.0 0.7 %copy-done.3 = bf16[64,64]{1,0:T(8,128)(2,1)S(1)} copy-done((bf16[64,64]{1,0:T(8,128)(2,1)S(1)}, bf16[64,64]{1,0:T(8,128)(2,1)}, u32[]{:S(2)}) %copy-start.3) | copy-done | bytes 8216
  5.7 0.0 copy-start.4
  5.7 0.7 %copy-done.4 = bf16[32,256]{1,0:T(8,128)(2,1)S(1)} copy-done((bf16[32,256]{1,0:T(8,128)(2,1)S(1)}, bf16[32,256]{1,0:T(8,128)(2,1)}, u32[]{:S(2)}) %copy-start.4) | copy-done | bytes 16408
  6.4 9.3 %front.1 = (bf16[1024,512]{1,0:T(8,128)(2,1)S(1)}, bf16[1024,4096]{1,0:T(8,128)(2,1)}) custom-call(bf16[1024,1024]{1,0:T(8,128)(2,1)S(1)} %copy-done, bf16[64,64]{1,0:T(8,128)(2,1)S(1)} %copy-done.3, bf16[32,256]{1,0:T(8,128)(2,1)S(1)} %copy-done.4), custom_call_target="tpu_custom_call" | custom-call | tf_op jit(solution)/shard_map/front/pallas_call | solution.py:61
  15.7 0.0 copy-start.1
  15.7 1.0 %copy-done.1 = bf16[1024,512]{1,0:T(8,128)(2,1)} copy-done((bf16[1024,512]{1,0:T(8,128)(2,1)}, bf16[1024,512]{1,0:T(8,128)(2,1)S(1)}, u32[]{:S(2)}) %copy-start.1) | copy-done | bytes 1048600
  16.7 0.0 copy-start.2
  16.7 0.9 %copy-done.2 = bf16[64,960]{1,0:T(8,128)(2,1)S(1)} copy-done((bf16[64,960]{1,0:T(8,128)(2,1)S(1)}, bf16[64,960]{1,0:T(8,128)(2,1)}, u32[]{:S(2)}) %copy-start.2) | copy-done | bytes 122904
  17.6 0.0 copy-start.5
  17.6 0.7 %copy-done.5 = s32[1,17]{1,0:T(1,128)S(1)} copy-done((s32[1,17]{1,0:T(1,128)S(1)}, s32[1,17]{1,0:T(1,128)}, u32[]{:S(2)}) %copy-start.5) | copy-done | bytes 92
  18.3 0.0 copy-start.6
  18.3 0.7 %copy-done.6 = s32[1,15]{1,0:T(1,128)S(1)} copy-done((s32[1,15]{1,0:T(1,128)S(1)}, s32[1,15]{1,0:T(1,128)}, u32[]{:S(2)}) %copy-start.6) | copy-done | bytes 84
  18.9 45.0 %hops.1 = bf16[1024,512]{1,0:T(8,128)(2,1)S(1)} custom-call(bf16[1024,512]{1,0:T(8,128)(2,1)} %copy-done.1, bf16[1024,1024]{1,0:T(8,128)(2,1)} %feat.1, bf16[1024,192]{1,0:T(8,128)(2,1)S(1)} %copy.11.band, bf16[64,960]{1,0:T(8,128)(2,1)S(1)} %copy-done.2, bf16[96,32]{1,0:T(8,128)(2,1)S(1)} %copy.12.mix, s32[1,17]{1,0:T(1,128)S(1)} %copy-done.5, ...), custom_call_target="tpu_custom_call" | custom-call | tf_op jit(solution)/shard_map/hops/pallas_call | solution.py:320
  63.9 1.0 %copy.15 = bf16[1024,512]{1,0:T(8,128)(2,1)} copy(bf16[1024,512]{1,0:T(8,128)(2,1)S(1)} %hops.1) | data formatting | bytes 2097152
Async XLA Ops:
  3.4 1.6 %copy-start = (bf16[1024,1024]{1,0:T(8,128)(2,1)S(1)}, bf16[1024,1024]{1,0:T(8,128)(2,1)}, u32[]{:S(2)}) copy-start(bf16[1024,1024]{1,0:T(8,128)(2,1)} %feat.1) | copy-start | bytes 6291460
  5.0 0.7 %copy-start.3 = (bf16[64,64]{1,0:T(8,128)(2,1)S(1)}, bf16[64,64]{1,0:T(8,128)(2,1)}, u32[]{:S(2)}) copy-start(bf16[64,64]{1,0:T(8,128)(2,1)} %fg_ref.1) | copy-start | bytes 24580
  5.7 0.7 %copy-start.4 = (bf16[32,256]{1,0:T(8,128)(2,1)S(1)}, bf16[32,256]{1,0:T(8,128)(2,1)}, u32[]{:S(2)}) copy-start(bf16[32,256]{1,0:T(8,128)(2,1)} %skip_ref.1) | copy-start | bytes 49156
  15.7 1.0 %copy-start.1 = (bf16[1024,512]{1,0:T(8,128)(2,1)}, bf16[1024,512]{1,0:T(8,128)(2,1)S(1)}, u32[]{:S(2)}) copy-start(bf16[1024,512]{1,0:T(8,128)(2,1)S(1)} %get-tuple-element.4.hid) | copy-start | bytes 3145732
  16.7 0.9 %copy-start.2 = (bf16[64,960]{1,0:T(8,128)(2,1)S(1)}, bf16[64,960]{1,0:T(8,128)(2,1)}, u32[]{:S(2)}) copy-start(bf16[64,960]{1,0:T(8,128)(2,1)} %farw.1) | copy-start | bytes 368644
  17.6 0.7 %copy-start.5 = (s32[1,17]{1,0:T(1,128)S(1)}, s32[1,17]{1,0:T(1,128)}, u32[]{:S(2)}) copy-start(s32[1,17]{1,0:T(1,128)} %ptr.1) | copy-start | bytes 208
  18.3 0.7 %copy-start.6 = (s32[1,15]{1,0:T(1,128)S(1)}, s32[1,15]{1,0:T(1,128)}, u32[]{:S(2)}) copy-start(s32[1,15]{1,0:T(1,128)} %col.1) | copy-start | bytes 184

commit v2 on v1

--- a/solution.py
+++ b/solution.py
@@ -75,7 +75,7 @@
             jax.ShapeDtypeStruct((rows, TOUT * S), BF16),
         ],
         scratch_shapes=[pltpu.VMEM((8 * CH, 8 * CH), BF16), pltpu.VMEM((4 * CH, 4 * S), BF16)],
-        compiler_params=pltpu.CompilerParams(vmem_limit_bytes=32 * 2**20),
+        compiler_params=pltpu.CompilerParams(vmem_limit_bytes=60 * 2**20),
         name="front",
     )(features, fg, skip)
 
@@ -125,7 +125,7 @@
 
     def stage(p, h):
         for e in range(EXPORT):
-            gat[p][h][me * EXPORT + e] = fld[p, h, exports[me, e] + 1]
+            gat[p][h][me * EXPORT + e] = fld[p, h, exports[e, me] + 1]
 
     stage(0, 0)
     pl.semaphore_wait(barrier, len(greet))
@@ -221,18 +221,22 @@
     def build():
         for r in range(blocks):
             i = r % GROUP
+            lines = slice(r * BLK, (r + 1) * BLK)
+            if i == 0:
+                high = jnp.transpose(band[:, r * BLK : (r + GROUP) * BLK])
             shift = one_hot((3 * BLK, (GROUP + 2) * BLK), lambda a, b: a + i * BLK == b)
-            lines = slice(r * BLK, (r + 1) * BLK)
-            band_mat[lines, :] = dot(band[lines, :], shift).astype(BF16)
+            band_mat[lines, :] = dot(high[i * BLK : (i + 1) * BLK, :], shift).astype(BF16)
             slot = lax.broadcasted_iota(jnp.int32, (1, slots * BLK), 1) // BLK
             used = jnp.logical_and(slot >= ptr[0, r], slot < ptr[0, r + 1])
             far_mat[lines, :] = farw[...] * jnp.where(used, 1.0, 0.0).astype(BF16)
         size = mix_wide.shape[1]
-        tall_rule = one_hot((size, CH), lambda a, b: a % CH == b)
         wide_rule = one_hot((CH, size), lambda a, b: a == b % CH)
         keep = one_hot((size, size), lambda a, b: a // CH == b // CH)
         for term in range(3):
-            tall = dot(tall_rule, mix[term * CH : (term + 1) * CH, :]).astype(BF16)
+            rule = one_hot((size, 3 * CH), lambda a, b: a % CH + term * CH == b)
+            tall = lax.dot_general(
+                rule, mix[...], (((1,), (1,)), ((), ())), preferred_element_type=F32
+            ).astype(BF16)
             mix_wide[term] = dot(tall, wide_rule).astype(BF16) * keep
 
     def hop_one(h):
@@ -339,10 +343,10 @@
             pltpu.SemaphoreType.DMA((1,)),
         ],
         compiler_params=pltpu.CompilerParams(
-            collective_id=0, has_side_effects=True, vmem_limit_bytes=52 * 2**20
+            collective_id=0, has_side_effects=True, vmem_limit_bytes=60 * 2**20
         ),
         name="hops",
-    )(hidden, features, band, farw, mix, ptr, col, exports)
+    )(hidden, features, band.T, farw, mix.T, ptr, col, exports.T)
 
 
 def solution(mesh):

time: 65.3 us -> 59.9 us (0.917)
  local copies, waits for them, and re-layouts: 9.93 us -> 2.26 us
  Pallas kernels: 54.3 us -> 56.6 us
    unnamed x18 -> x1, local copies, waits for them, and re-layouts: 9.93 us -> 2.26 us
    pallas_call x1, Pallas kernels: 9.31 us -> 10.8 us  [front(): pl.pallas_call(front_kernel, grid=(rows // tile,), in_specs=[pl.BlockSpec...]
    pallas_call x1, Pallas kernels: 45 us -> 45.8 us  [hops(): pl.pallas_call(functools.partial(hops_kernel, n, zs, ys), in_specs=[vmem,...]
where the time goes in v2:
time: 59.9 us; the launch traced here: 59.5 us
  Pallas kernels  56.6 us (94%)
  local copies, waits for them, and re-layouts  2.26 us (4%)
  between operations  0.64 us (1%)
    pallas_call x1, Pallas kernels, hops(): pl.pallas_call(functools.partial(hops_kernel, n, zs, ys), in_specs=[vmem,...  45.8 us
    pallas_call x1, Pallas kernels, front(): pl.pallas_call(front_kernel, grid=(rows // tile,), in_specs=[pl.BlockSpec...  10.8 us
    unnamed x1, local copies, waits for them, and re-layouts  2.26 us

profile of v2, /device:TPU:1, one launch (start us, length us, event | category | flops | bytes accessed | tf_op | source)
XLA Modules:
  0.0 59.5 jit_solution(8499824045767076907)
XLA Ops:
  0.6 10.8 %front.1 = (bf16[1024,512]{1,0:T(8,128)(2,1)}, bf16[1024,4096]{1,0:T(8,128)(2,1)}) custom-call(bf16[1024,1024]{1,0:T(8,128)(2,1)} %feat.1, bf16[64,64]{1,0:T(8,128)(2,1)} %fg_ref.1, bf16[32,256]{1,0:T(8,128)(2,1)} %skip_ref.1), custom_call_target="tpu_custom_call" | custom-call | tf_op jit(solution)/shard_map/front/pallas_call | solution.py:61
  11.4 45.8 %hops.1 = bf16[1024,512]{1,0:T(8,128)(2,1)} custom-call(bf16[1024,512]{1,0:T(8,128)(2,1)} %get-tuple-element.4.hid, bf16[1024,1024]{1,0:T(8,128)(2,1)} %feat.1, bf16[192,1024]{1,0:T(8,128)(2,1)} %bitcast.3, bf16[64,960]{1,0:T(8,128)(2,1)} %farw.1, bf16[32,96]{1,0:T(8,128)(2,1)} %bitcast.4, s32[1,17]{1,0:T(1,128)} %ptr.1, s32[1,15]{1,0:T(1,128)} %col.1, ...), custom_call_target="tpu_custom_call" | custom-call | tf_op jit(solution)/shard_map/hops/pallas_call | solution.py:324
  57.3 2.3 %copy.12 = bf16[1024,512]{1,0:T(8,128)(2,1)} copy(bf16[1024,512]{1,0:T(8,128)(2,1)} %hops.1) | data formatting | bytes 2097152
